TPU v7x, 256 devices: a whole 4x4x8 slice. The times are simulated.
256 devices in a mesh: seq: 8 (over z), tp: 8 (over y_hi, x), rep: 4 (over y_lo, core).
Axes of the slice: x: 4, y: 4 (y_hi: 2, y_lo: 2; y = y_hi * 2 + y_lo), z: 8, core: 2. Of those that a mesh axis runs over, the one named last changes fastest.
Arguments:
- query_span: bfloat16 [4096, 8192], P(('seq', 'rep'), 'tp'), may hold values from -20 to 20
- key_span: bfloat16 [4096, 1024], P(('seq', 'rep'), 'tp'), may hold values from -5 to 5
- value_span: bfloat16 [4096, 1024], P(('seq', 'rep'), 'tp'), may hold values from -5 to 5
- context_keys: bfloat16 [16384, 1024], P(('seq', 'rep'), 'tp'), may hold values from -4 to 4
- context_values: bfloat16 [16384, 1024], P(('seq', 'rep'), 'tp'), may hold values from -5 to 5
- span_offset: int32 [1], replicated, may hold values from 8192 to 16384
- decode_query: bfloat16 [8, 128, 2048], P('tp', ('seq', 'rep')), may hold values from -20 to 20
- lengths: int32 [2, 128], P(None, ('seq', 'rep')), may hold values from 128 to 512, as said below
- slot_table: int32 [2, 128], P(None, ('seq', 'rep')), may hold values from 0 to 5, as said below
- cache_keys: bfloat16 [8, 192, 512, 256], P('tp', ('seq', 'rep')), may hold values from -4 to 4
- cache_values: bfloat16 [8, 192, 512, 256], P('tp', ('seq', 'rep')), may hold values from -5 to 5
Outputs:
- attended: bfloat16 [4096, 8192], P(('seq', 'rep'), 'tp')
- handed: bfloat16 [8, 2048, 512], P('tp', ('seq', 'rep'))
- decoded: bfloat16 [8, 128, 2048], P('tp', ('seq', 'rep'))
Inputs may be any that keep to these rules, and one draw needn't show every extreme that they name: `lengths`: some request has exactly 512 cached positions and some has 128. `slot_table`: the 4 requests of one half in one block of 4 requests have distinct slots.
All inputs are finite; a program needn't handle non-finite values.
Results may differ from a plain program's by a relative error of at most 0.007.
Values may be sent and summed in bfloat16 or wider, within the bound.
A program may use at most 64 MiB of HBM per device.

v0:
```python
import jax
import jax.numpy as jnp
from jax import lax
from jax.sharding import PartitionSpec as P

H = 64
KVH = 8
HD = 128


NEG_BIG = -1e30


def swapped(x, axis, distance):
    return lax.ppermute(x, axis, [(i, i ^ 1 << distance) for i in range(lax.axis_size(axis))])


def key_layout(row_count, first_row, shard_rows, ctx_rows, query_rows, stride, column):
    global_rows = first_row + jnp.arange(row_count, dtype=jnp.int32)
    shard_num = global_rows // shard_rows
    within = global_rows - shard_num * shard_rows
    block_index = shard_num * stride + column
    is_ctx = within < ctx_rows
    ctx_pos = block_index * ctx_rows + within
    span_row = block_index * query_rows + within - ctx_rows
    return (is_ctx, ctx_pos, span_row)


def fold_block(state, queries, row_ids, kv_block, layout, valid_limit):
    run_max, run_sum, run_acc = state
    is_ctx, ctx_pos, span_row = layout
    heads_kv = run_max.shape[0]
    head_dim = run_acc.shape[3]
    half_width = kv_block.shape[1] // 2
    key_rows = kv_block[:, :half_width].reshape(kv_block.shape[0], heads_kv, head_dim)
    value_rows = kv_block[:, half_width:].reshape(kv_block.shape[0], heads_kv, head_dim)
    scores = jnp.einsum(
        "qegd,ned->egqn", queries, key_rows, preferred_element_type=jnp.float32
    ) * head_dim ** (-0.5)
    is_valid = jnp.where(
        is_ctx[None, :], ctx_pos[None, :] < valid_limit, span_row[None, :] <= row_ids[:, None]
    )
    is_valid = is_valid[None, None]
    masked = jnp.where(is_valid, scores, NEG_BIG)
    new_max = jnp.maximum(run_max, jnp.max(masked, axis=-1))
    weights = jnp.where(is_valid, jnp.exp(scores - new_max[..., None]), 0.0)
    factor = jnp.exp(run_max - new_max)
    new_sum = run_sum * factor + jnp.sum(weights, axis=-1)
    product = jnp.einsum(
        "egqn,ned->egqd",
        weights.astype(jnp.bfloat16),
        value_rows,
        preferred_element_type=jnp.float32,
    )
    new_acc = run_acc * factor[..., None] + product
    return (new_max, new_sum, new_acc)


def make_fold(queries, row_ids, valid_limit, shard_rows, ctx_rows, query_rows, stride, column):

    def folder(state, shard_piece, first_row):
        row_count = shard_piece.shape[0]
        sub_steps = max(row_count // shard_rows, 1)
        sub_rows = row_count // sub_steps

        def one_step(position, inner_state):
            kv_block = lax.dynamic_slice_in_dim(shard_piece, position * sub_rows, sub_rows, 0)
            layout = key_layout(
                sub_rows, position * sub_rows, shard_rows, ctx_rows, query_rows, stride, column
            )
            return fold_block(inner_state, queries, row_ids, kv_block, layout, valid_limit)

        return lax.fori_loop(0, sub_steps, one_step, state)

    return folder


def initial(heads_kv, groups, row_count, head_dim):
    return (
        jnp.full((heads_kv, groups, row_count), NEG_BIG, jnp.float32),
        jnp.zeros((heads_kv, groups, row_count), jnp.float32),
        jnp.zeros((heads_kv, groups, row_count, head_dim), jnp.float32),
    )


def on_device(
    query_span,
    key_span,
    value_span,
    context_keys,
    context_values,
    span_offset,
    decode_query,
    lengths,
    slot_table,
    cache_keys,
    cache_values,
):
    query_rows = query_span.shape[0]
    ctx_rows = context_keys.shape[0]
    heads_kv = key_span.shape[1] // HD
    groups = H // KVH
    shard_rows = ctx_rows + query_rows
    valid_limit = span_offset[0]
    span_kv = jnp.concatenate([key_span, value_span], axis=1)
    local_kv = jnp.concatenate(
        [jnp.concatenate([context_keys, context_values], axis=1), span_kv], axis=0
    )
    block_index = lax.axis_index(("seq", "rep"))
    row_ids = block_index * query_rows + jnp.arange(query_rows, dtype=jnp.int32)
    queries = query_span.reshape(query_rows, heads_kv, groups, HD)
    folder = make_fold(queries, row_ids, valid_limit, shard_rows, ctx_rows, query_rows, 1, 0)
    run_max, run_sum, run_acc = folder(
        initial(heads_kv, groups, query_rows, HD),
        lax.all_gather(local_kv, ("seq", "rep"), axis=0, tiled=True),
        jnp.int32(0),
    )
    result = run_acc / run_sum[..., None]
    attended = (
        jnp.transpose(result, (2, 0, 1, 3))
        .reshape(query_rows, heads_kv * groups * HD)
        .astype(jnp.bfloat16)
    )
    tp_count = lax.axis_size("tp")
    half_index = lax.axis_index("tp") // (tp_count // 2)
    half_rows = query_rows // 2
    kept_rows = lax.dynamic_slice_in_dim(span_kv, half_index * half_rows, half_rows, 0)
    sent_rows = lax.dynamic_slice_in_dim(span_kv, (1 - half_index) * half_rows, half_rows, 0)
    received = swapped(sent_rows, "tp", tp_count.bit_length() - 2)
    lower_part = jnp.where(half_index == 0, kept_rows, received)
    upper_part = jnp.where(half_index == 0, received, kept_rows)
    handed = jnp.concatenate([lower_part, upper_part], axis=1)[None]
    live_len = lax.dynamic_index_in_dim(lengths, half_index, 0, keepdims=False)
    slot_picks = lax.dynamic_index_in_dim(slot_table, half_index, 0, keepdims=False)
    requests = decode_query.shape[1]
    cache_len = cache_keys.shape[2]
    pair_heads = cache_keys.shape[3] // HD
    key_rows = jnp.take(cache_keys[0], slot_picks, axis=0).reshape(
        requests, cache_len, pair_heads, HD
    )
    value_rows = jnp.take(cache_values[0], slot_picks, axis=0).reshape(
        requests, cache_len, pair_heads, HD
    )
    dec_queries = decode_query[0].reshape(requests, pair_heads, groups, HD)
    scores = jnp.einsum(
        "bhgd,blhd->bhgl", dec_queries, key_rows, preferred_element_type=jnp.float32
    ) * HD ** (-0.5)
    is_valid = (jnp.arange(cache_len, dtype=jnp.int32)[None, :] < live_len[:, None])[
        :, None, None, :
    ]
    row_max = jnp.max(jnp.where(is_valid, scores, NEG_BIG), axis=-1)
    weights = jnp.where(is_valid, jnp.exp(scores - row_max[..., None]), 0.0)
    weight_sum = jnp.sum(weights, axis=-1)
    mixed_out = jnp.einsum(
        "bhgl,blhd->bhgd",
        weights.astype(jnp.bfloat16),
        value_rows,
        preferred_element_type=jnp.float32,
    )
    decoded = (
        (mixed_out / weight_sum[..., None])
        .reshape(1, requests, pair_heads * groups * HD)
        .astype(jnp.bfloat16)
    )
    return (attended, handed, decoded)


def solution(mesh):
    placed = (
        P(("seq", "rep"), "tp"),
        P(("seq", "rep"), "tp"),
        P(("seq", "rep"), "tp"),
        P(("seq", "rep"), "tp"),
        P(("seq", "rep"), "tp"),
        P(),
        P("tp", ("seq", "rep"), None),
        P(None, ("seq", "rep")),
        P(None, ("seq", "rep")),
        P("tp", ("seq", "rep"), None, None),
        P("tp", ("seq", "rep"), None, None),
    )
    return jax.shard_map(
        on_device,
        mesh=mesh,
        in_specs=placed,
        out_specs=(
            P(("seq", "rep"), "tp"),
            P("tp", ("seq", "rep"), None),
            P("tp", ("seq", "rep"), None),
        ),
        check_vma=False,
    )
```

profile of v0, /device:TPU:1, one launch (start us, length us, event | category | flops | bytes accessed | tf_op | source)
XLA Modules:
  0.0 387.4 jit_solution(2531373935480668549)
XLA Ops:
  10.7 3.8 collective-permute-start
  15.8 3.0 gather_fusion.1
  23.0 66.9 %all-gather.2.cloned.1.call-done = bf16[20480,256]{1,0:T(8,128)(2,1)} async-done(((bf16[640,256]{1,0:T(8,128)(2,1)}), bf16[20480,256]{1,0:T(8,128)(2,1)}) %all-gather.2.cloned.1.call-update) | async-done | bytes 10485776 | tf_op jit(solution)/shard_map/all_gather | solution.py:115
  89.9 289.5 %while.20 = (s32[]{:T(128)}, f32[1,8,128]{2,1,0:T(8,128)S(1)}, f32[1,8,128]{2,1,0:T(8,128)S(1)}, f32[1,8,128,128]{3,2,1,0:T(8,128)S(1)}, s32[]{:T(128)}, /*index...) while((s32[]{:T(128)}, f32[1,8,128]{2,1,0:T(8,128)S(1)}, ...), condition=%wide.region_3.4_spmd.clone, body=%wide.region_0.3_spmd.clone.sunk | while | flops 343335168 | bytes 9904871 | solution.py:73
  90.9 3.0 fusion.53
  96.2 2.7 fusion.56
  100.0 3.0 fusion.53
  105.3 2.7 fusion.56
  109.0 3.0 fusion.53
  114.3 2.7 fusion.56
  118.1 3.0 fusion.53
  123.4 2.7 fusion.56
  127.1 3.0 fusion.53
  132.4 2.7 fusion.56
  136.2 3.0 fusion.53
  141.5 2.7 fusion.56
  145.2 3.0 fusion.53
  150.5 2.7 fusion.56
  154.3 3.0 fusion.53
  159.6 2.7 fusion.56
  163.3 3.0 fusion.53
  168.6 2.7 fusion.56
  172.4 3.0 fusion.53
  177.7 2.7 fusion.56
  181.4 3.0 fusion.53
  186.7 2.7 fusion.56
  190.5 3.0 fusion.53
  195.8 2.7 fusion.56
  199.5 3.0 fusion.53
  204.8 2.7 fusion.56
  208.6 3.0 fusion.53
  213.9 2.7 fusion.56
  217.6 3.0 fusion.53
  222.9 2.7 fusion.56
  226.7 3.0 fusion.53
  232.0 2.7 fusion.56
  235.7 3.0 fusion.53
  241.0 2.7 fusion.56
  244.8 3.0 fusion.53
  250.1 2.7 fusion.56
  253.8 3.0 fusion.53
  259.1 2.7 fusion.56
  262.8 3.0 fusion.53
  268.2 2.7 fusion.56
  271.9 3.0 fusion.53
  277.2 2.7 fusion.56
  280.9 3.0 fusion.53
  286.3 2.7 fusion.56
  290.0 3.0 fusion.53
  295.3 2.7 fusion.56
  299.0 3.0 fusion.53
  304.3 2.7 fusion.56
  308.1 3.0 fusion.53
  317.1 3.0 fusion.53
  322.4 2.7 fusion.56
  326.2 3.0 fusion.53
  335.2 3.0 fusion.53
  340.5 2.7 fusion.56
  344.3 3.0 fusion.53
  353.3 3.0 fusion.53
  358.6 2.7 fusion.56
  362.4 3.0 fusion.53
  371.4 3.0 fusion.53
  376.7 2.7 fusion.56
  (295 shorter events, 126.9 us)
Async XLA Ops:
  7.2 8.0 %copy-start = (bf16[1,6,512,256]{3,2,1,0:T(8,128)(2,1)S(1)}, bf16[1,6,512,256]{3,2,1,0:T(8,128)(2,1)}, u32[]{:S(2)}) copy-start(bf16[1,6,512,256]{3,2,1,0:T(8,128)(2,1)} %param.24) | copy-start | bytes 4718596
  7.2 82.7 %all-gather.2.cloned.1.call-start = ((), (), s32[]{:S(2)}) async-start(), calls=%async_computation | async-start | bytes 10813440 | tf_op jit(solution)/shard_map/all_gather | solution.py:115
  8.9 10.0 %copy-start.3 = (s32[2,4]{1,0:T(2,128)S(1)}, s32[2,4]{1,0:T(2,128)}, u32[]{:S(2)}) copy-start(s32[2,4]{1,0:T(2,128)} %param.22) | copy-start | bytes 100
  10.7 11.6 %collective-permute-start = (bf16[64,256]{1,0:T(8,128)(2,1)S(1)}, bf16[64,256]{1,0:T(8,128)(2,1)S(1)}, u32[]{:S(2)}, u32[]{:S(2)}) collective-permute-start(bf16[64,256]{1,0:T(8,128)(2,1)S(1)} %constant_dynamic-slice_fusion.2), channel_id=1, source_target_pairs={{0,16},{4,20},{8,24},{12,28},{16,0},{20,4},{24,8},{28,12},{1,17},{... | collective-permute-start | bytes 98312 | tf_op jit(solution)/shard_map/ppermute | solution.py:15
  18.8 1.6 copy-start.2
  18.9 2.4 copy-start.1
Sparse Core Ops, SparseCore 0:
  10.8 79.0 all-gather.1
where the time goes:
time: 391 us; the launch traced here: 387 us
  matrix products  182 us (47%)
  other arithmetic  111 us (28%)
  waiting for transfers between devices  66.9 us (17%)
  between operations  14.2 us (4%)
  local copies, waits for them, and re-layouts  7.27 us (2%)
    dot_general x32, matrix products, fold_block(): jnp.einsum('qegd,ned->egqn', queries, key_rows, preferred_element_type=jn...  95.3 us
    dot_general x32, matrix products, fold_block(): jnp.einsum('egqn,ned->egqd', weights.astype(jnp.bfloat16), value_rows, pr...  85.8 us
    reduce_sum x32, other arithmetic, fold_block(): new_sum = run_sum * factor + jnp.sum(weights, axis=-1)  73.1 us
    all_gather x1, waiting for transfers between devices, on_device(): lax.all_gather(local_kv, ('seq', 'rep'), axis=0, tiled=True)  66.9 us
    lt x32, other arithmetic, fold_block(): ctx_pos[None, :] < valid_limit  21.3 us
    select_n x32, other arithmetic, fold_block(): jnp.where(is_ctx[None, :], ctx_pos[None, :] < valid_limit, span_row[None,...  10.3 us
  transfers between devices with their start and end apart: 2, of which 1 were waited for; matrix products, arithmetic and copies ran while one was open for 2% of the time, Pallas kernels for 0%

commit v1 on v0

v1 whole, which is shorter than its diff:
```python
import jax
import jax.numpy as jnp
from jax import lax
from jax.experimental import pallas as pl
from jax.experimental.pallas import tpu as pltpu
from jax.sharding import PartitionSpec as P

HD = 128
GROUPS = 8
QROWS = 128
CROWS = 512
Z = 8
SCALE2 = 1.4426950408889634 / 128**0.5
MASKED = -1e31
M_START = -1e29
SPAN_BASE = 7168
LAST_BASE = 9216
ALL_ROWS = 10240
TILE = 256
MESH = pl.DeviceIdType.MESH
BF = jnp.bfloat16
F32 = jnp.float32

CK, CV, SK, SV = range(4)
SLOT_OF = ((0, 1, 3, 5, 7), (0, 2, 4, 6, 7))

STEPS = (
    (0, 0, 1024),
    (1, 0, 1024),
    (1, 1024, 2048),
    (0, 1024, 2048),
    (1, SPAN_BASE, 2048),
    (0, SPAN_BASE, 2048),
    (1, 3072, 2048),
    (0, 3072, 2048),
    (1, 5120, 2048),
    (1, LAST_BASE, 1024),
    (0, 5120, 2048),
    (0, LAST_BASE, 1024),
)
SEND_AFTER = 9


def pick(i, table):
    total = jnp.int32(0)
    for at, value in enumerate(table):
        if value:
            total = total + jnp.where(i == at, jnp.int32(value), jnp.int32(0))
    return total


def kernel(
    query,
    key_span,
    value_span,
    ctx_k,
    ctx_v,
    offset,
    dec_q,
    lengths,
    slots,
    cache_k,
    cache_v,
    out_att,
    out_hand,
    out_dec,
    qb,
    kall,
    vall,
    mask,
    ident,
    m_ref,
    acc_ref,
    o_send,
    o_recv,
    l_send,
    l_recv,
    hbuf,
    dqb,
    ckb,
    cvb,
    ring_send,
    ring_recv,
    core_send,
    core_recv,
    misc_send,
    misc_recv,
    local_sem,
):
    z = lax.axis_index("seq")
    tp = lax.axis_index("tp")
    rep = lax.axis_index("rep")
    y = rep // 2
    c = rep % 2
    half = tp // 4
    nxt = {"seq": (z + 1) % Z}
    prv = {"seq": (z + Z - 1) % Z}
    core = {"rep": y * 2 + (1 - c)}
    other = {"rep": (1 - y) * 2 + c}
    mate = {"tp": (1 - half) * 4 + tp % 4}

    def rows(slot, kind, which):
        if kind in (CK, CV):
            base = slot * 1024 if slot < 7 else LAST_BASE
            return pl.ds(pl.multiple_of(base + which * CROWS, CROWS), CROWS)
        return pl.ds(pl.multiple_of(SPAN_BASE + slot * 256 + which * QROWS, QROWS), QROWS)

    def held(slot, kind, which):
        ref = kall if kind in (CK, SK) else vall
        return ref.at[rows(slot, kind, which), :]

    own = (ctx_k, ctx_v, key_span, value_span)

    def ring(way, hop, kind):
        src = own[kind] if hop == 1 else held(SLOT_OF[way][hop - 1], kind, c)
        at = (way * 4 + hop - 1) * 4 + kind
        return pltpu.make_async_remote_copy(
            src_ref=src,
            dst_ref=held(SLOT_OF[way][hop], kind, c),
            send_sem=ring_send.at[at],
            recv_sem=ring_recv.at[at],
            device_id=nxt if way == 0 else prv,
            device_id_type=MESH,
        )

    def has_hop(way, hop, kind):
        return hop <= 3 or (hop == 4 and (kind in (CK, SK)) == (way == 0))

    def across(slot, kind, incoming=False):
        at = slot * 4 + kind
        return pltpu.make_async_remote_copy(
            src_ref=own[kind] if slot == 0 else held(slot, kind, c),
            dst_ref=held(slot, kind, 1 - c if incoming else c),
            send_sem=core_send.at[at],
            recv_sem=core_recv.at[at],
            device_id=core,
            device_id_type=MESH,
        )

    def pass_on(hop, kind):
        for way in (0, 1):
            if has_hop(way, hop, kind):
                ring(way, hop, kind).wait_recv()
                if has_hop(way, hop + 1, kind):
                    ring(way, hop + 1, kind).start()
                across(SLOT_OF[way][hop], kind).start()

    def from_core(slot_list, kinds):
        for slot in slot_list:
            for kind in kinds:
                across(slot, kind, True).wait_recv()

    def misc(at, src, dst, device):
        return pltpu.make_async_remote_copy(
            src_ref=src,
            dst_ref=dst,
            send_sem=misc_send.at[at],
            recv_sem=misc_recv.at[at],
            device_id=device,
            device_id_type=MESH,
        )

    q_copy = misc(0, query, qb.at[1], other)
    kept = pl.ds(pl.multiple_of(half * 64, 64), 64)
    given = pl.ds(pl.multiple_of((1 - half) * 64, 64), 64)
    hk_copy = misc(1, key_span.at[given, :], hbuf.at[half, 0], mate)
    hv_copy = misc(2, value_span.at[given, :], hbuf.at[half, 1], mate)
    o_copy = misc(3, o_send, o_recv, other)
    l_copy = misc(4, l_send, l_recv, other)

    local = [
        pltpu.make_async_copy(src, dst, local_sem.at[at])
        for at, (src, dst) in enumerate(
            (
                (query, qb.at[0]),
                (ctx_k, held(0, CK, c)),
                (ctx_v, held(0, CV, c)),
                (key_span, held(0, SK, c)),
                (value_span, held(0, SV, c)),
                (dec_q.at[0], dqb),
                (cache_k.at[0], ckb),
                (cache_v.at[0], cvb),
                (key_span.at[kept, :], hbuf.at[half, 0]),
                (value_span.at[kept, :], hbuf.at[half, 1]),
            )
        )
    ]
    barrier = pltpu.get_barrier_semaphore()
    for device in (nxt, prv, core, other, mate):
        pl.semaphore_signal(barrier, inc=1, device_id=device, device_id_type=MESH)
    for copy in local:
        copy.start()
    pl.semaphore_wait(barrier, 5)

    for kind in (SK, SV, CK):
        for way in (0, 1):
            ring(way, 1, kind).start()
    for kind in (CK, CV, SK, SV):
        across(0, kind).start()
    q_copy.start()
    hk_copy.start()
    hv_copy.start()

    row = lax.broadcasted_iota(jnp.int32, (QROWS, HD), 0)
    col = lax.broadcasted_iota(jnp.int32, (QROWS, HD), 1)
    ident[...] = jnp.where(row == col, 1.0, 0.0).astype(BF)
    limit = offset[0]
    long_row = lax.broadcasted_iota(jnp.int32, (CROWS, HD), 0)

    def fill(slot, carry):
        odd = slot % 2
        z_slot = (z + 2 * Z - odd * ((slot + 1) // 2) + (1 - odd) * (slot // 2)) % Z
        for which in (0, 1):
            block = z_slot * 4 + y * 2 + which
            base = slot * 1024 + jnp.where(slot == 7, LAST_BASE - SPAN_BASE, 0) + which * CROWS
            mask[pl.ds(pl.multiple_of(base, CROWS), CROWS), :] = jnp.where(
                long_row + block * CROWS >= limit, MASKED, 0.0
            ).astype(BF)
            for b in (0, 1):
                y_b = y if b == 0 else 1 - y
                ahead = (block - (z * 4 + y_b * 2 + c)) * QROWS
                base = (SPAN_BASE if b == 0 else ALL_ROWS) + slot * 256 + which * QROWS
                mask[pl.ds(pl.multiple_of(base, QROWS), QROWS), :] = jnp.where(
                    row + ahead > col, MASKED, 0.0
                ).astype(BF)
        return carry

    lax.fori_loop(0, 8, fill, 0)
    m_ref[...] = jnp.full_like(m_ref, M_START)
    acc_ref[...] = jnp.zeros_like(acc_ref)

    for kind in (SK, SV):
        pass_on(1, kind)
    for way in (0, 1):
        ring(way, 1, CV).start()

    for copy in local:
        copy.wait()
    dq = dqb[...].astype(F32)
    picked = [slots[half, b] for b in range(4)]
    live = [lengths[half, b] for b in range(4)]
    place = lax.broadcasted_iota(jnp.int32, (64, 512), 1)
    request = lax.broadcasted_iota(jnp.int32, (64, 512), 0) % 8
    ok = jnp.concatenate(
        [(request == b) & (place < live[b]) for b in range(4)], axis=1
    )
    blank = jnp.zeros((4, HD), F32)
    for head in (0, 1):
        lanes = slice(head * HD, (head + 1) * HD)
        q = jnp.concatenate(
            [
                part
                for g in range(GROUPS)
                for part in (dq[:, (head * 8 + g) * HD : (head * 8 + g + 1) * HD], blank)
            ],
            axis=0,
        ).astype(BF)
        k = jnp.concatenate([ckb[picked[b]][:, lanes] for b in range(4)], axis=0)
        v = jnp.concatenate([cvb[picked[b]][:, lanes] for b in range(4)], axis=0)
        s = lax.dot_general(q, k, (((1,), (1,)), ((), ())), preferred_element_type=F32)
        s = jnp.where(ok, s * SCALE2, MASKED)
        top = jnp.max(s, axis=1, keepdims=True)
        w = jnp.where(ok, jnp.exp2(s - top), 0.0)
        total = jnp.sum(w, axis=1, keepdims=True)
        o = lax.dot_general(
            w.astype(BF), v, (((1,), (0,)), ((), ())), preferred_element_type=F32
        )
        o = o / total
        for g in range(GROUPS):
            out_dec[0, :, (head * 8 + g) * HD : (head * 8 + g + 1) * HD] = o[
                g * 8 : g * 8 + 4, :
            ].astype(BF)

    for kind in (SK, SV):
        pass_on(2, kind)

    def scores_block(b, key_off, mask_off, width):
        keys = pl.ds(pl.multiple_of(key_off, 1024), width)
        k = jnp.concatenate(
            [kall[keys, :], mask[pl.ds(pl.multiple_of(mask_off, 1024), width), :]], axis=1
        )
        v = jnp.concatenate([vall[keys, :], jnp.ones((width, HD), BF)], axis=1)
        eye = jnp.concatenate([ident[...]] * 2, axis=0)
        all_s = []
        for t in range(4):
            q = jnp.concatenate(
                [qb[b, :, (2 * t + u) * HD : (2 * t + u + 1) * HD] for u in (0, 1)], axis=0
            )
            q = jnp.concatenate([q, eye], axis=1)
            all_s.append(
                lax.dot_general(q, k, (((1,), (1,)), ((), ())), preferred_element_type=F32)
            )
        for t in range(4):
            s = all_s[t]
            at = pl.ds(t * TILE, TILE)
            before = m_ref[b, at, :]
            now = jnp.maximum(before, jnp.max(s, axis=1, keepdims=True) * SCALE2)
            factor = jnp.exp2(before - now)
            p = jnp.exp2(s * SCALE2 - now[:, :1])
            m_ref[b, at, :] = now
            pv = lax.dot_general(
                p.astype(BF), v, (((1,), (0,)), ((), ())), preferred_element_type=F32
            )
            acc_ref[b, at, :] = acc_ref[b, at, :] * jnp.concatenate([factor, factor], axis=1) + pv

    def duties(step):
        if step == 0:
            from_core((0,), (CK, CV))
        elif step == 1:
            pass_on(3, SK)
            pass_on(3, SV)
            pass_on(1, CK)
            q_copy.wait_recv()
        elif step == 2:
            pass_on(4, SK)
            pass_on(4, SV)
            pass_on(1, CV)
            from_core((1, 2), (CK, CV))
        elif step == 4:
            pass_on(2, CK)
            from_core(range(8), (SK, SV))
        elif step == 5:
            pass_on(2, CV)
        elif step == 6:
            pass_on(3, CK)
            from_core((3, 4), (CK, CV))
        elif step == 7:
            pass_on(3, CV)
        elif step == 8:
            from_core((5, 6), (CK, CV))
        elif step == 9:
            pass_on(4, CK)
            pass_on(4, CV)
            from_core((7,), (CK, CV))

    def one_step(i, carry):
        for step in range(len(STEPS)):
            pl.when(i == step)(lambda step=step: duties(step))
        b = pick(i, [s[0] for s in STEPS])
        off = pick(i, [s[1] for s in STEPS])
        m_off = pick(
            i, [ALL_ROWS if s[0] == 1 and s[1] == SPAN_BASE else s[1] for s in STEPS]
        )
        short = pick(i, [int(s[2] == 1024) for s in STEPS])
        pl.when(short == 1)(lambda: scores_block(b, off, m_off, 1024))
        pl.when(short == 0)(lambda: scores_block(b, off, m_off, 2048))

        @pl.when(i == SEND_AFTER)
        def _():
            eye = ident[...].astype(F32)
            for g in range(GROUPS):
                at = pl.ds(g * QROWS, QROWS)
                total = acc_ref[1, at, HD:]
                o_send[at, :] = (acc_ref[1, at, :HD] / total).astype(BF)
                level = m_ref[1, at, :] + jnp.log(total) * 1.4426950408889634
                l_send[g : g + 1, :] = jnp.sum(level * eye, axis=0, keepdims=True)
            l_copy.start()
            o_copy.start()

        return carry

    lax.fori_loop(0, len(STEPS), one_step, 0)

    hk_copy.wait()
    hv_copy.wait()
    for u in (0, 1):
        for kv in (0, 1):
            out_hand[0, :, (u * 2 + kv) * HD : (u * 2 + kv + 1) * HD] = hbuf[u, kv]
    for way in (0, 1):
        for hop in (1, 2, 3, 4):
            for kind in range(4):
                if has_hop(way, hop, kind):
                    ring(way, hop, kind).wait_send()
    for slot in range(8):
        for kind in range(4):
            across(slot, kind).wait_send()
    q_copy.wait_send()
    l_copy.wait()
    o_copy.wait()
    eye = ident[...].astype(F32)
    for g in range(GROUPS):
        at = pl.ds(g * QROWS, QROWS)
        level = jnp.sum(eye * l_recv[g : g + 1, :], axis=1, keepdims=True)
        mine = m_ref[0, at, :]
        top = jnp.maximum(mine, level)
        w_mine = jnp.exp2(mine - top)
        w_other = jnp.exp2(level - top)
        total = acc_ref[0, at, HD:] * w_mine + w_other
        o = acc_ref[0, at, :HD] * w_mine + o_recv[at, :].astype(F32) * w_other
        out_att[:, g * HD : (g + 1) * HD] = (o / total).astype(BF)


def on_device(*args):
    anywhere = pl.BlockSpec(memory_space=pl.ANY)
    vmem = pl.BlockSpec(memory_space=pltpu.VMEM)
    smem = pl.BlockSpec(memory_space=pltpu.SMEM)
    dma = pltpu.SemaphoreType.DMA
    return pl.pallas_call(
        kernel,
        out_shape=(
            jax.ShapeDtypeStruct((QROWS, GROUPS * HD), BF),
            jax.ShapeDtypeStruct((1, 64, 512), BF),
            jax.ShapeDtypeStruct((1, 4, 2048), BF),
        ),
        in_specs=[
            anywhere,
            anywhere,
            anywhere,
            anywhere,
            anywhere,
            smem,
            anywhere,
            smem,
            smem,
            anywhere,
            anywhere,
        ],
        out_specs=(vmem, vmem, vmem),
        scratch_shapes=[
            pltpu.VMEM((2, QROWS, GROUPS * HD), BF),
            pltpu.VMEM((ALL_ROWS, HD), BF),
            pltpu.VMEM((ALL_ROWS, HD), BF),
            pltpu.VMEM((ALL_ROWS + 2048, HD), BF),
            pltpu.VMEM((QROWS, HD), BF),
            pltpu.VMEM((2, GROUPS * QROWS, HD), F32),
            pltpu.VMEM((2, GROUPS * QROWS, 2 * HD), F32),
            pltpu.VMEM((GROUPS * QROWS, HD), BF),
            pltpu.VMEM((GROUPS * QROWS, HD), BF),
            pltpu.VMEM((GROUPS, HD), F32),
            pltpu.VMEM((GROUPS, HD), F32),
            pltpu.VMEM((2, 2, 64, HD), BF),
            pltpu.VMEM((4, 2048), BF),
            pltpu.VMEM((6, 512, 256), BF),
            pltpu.VMEM((6, 512, 256), BF),
            dma((32,)),
            dma((32,)),
            dma((32,)),
            dma((32,)),
            dma((5,)),
            dma((5,)),
            dma((10,)),
        ],
        compiler_params=pltpu.CompilerParams(
            collective_id=0, has_side_effects=True, vmem_limit_bytes=56 * 2**20
        ),
        cost_estimate=pl.CostEstimate(
            flops=12 * 10**9, bytes_accessed=8 * 10**6, transcendentals=22 * 10**6
        ),
    )(*args)


def solution(mesh):
    placed = (
        P(("seq", "rep"), "tp"),
        P(("seq", "rep"), "tp"),
        P(("seq", "rep"), "tp"),
        P(("seq", "rep"), "tp"),
        P(("seq", "rep"), "tp"),
        P(),
        P("tp", ("seq", "rep"), None),
        P(None, ("seq", "rep")),
        P(None, ("seq", "rep")),
        P("tp", ("seq", "rep"), None, None),
        P("tp", ("seq", "rep"), None, None),
    )
    return jax.shard_map(
        on_device,
        mesh=mesh,
        in_specs=placed,
        out_specs=(
            P(("seq", "rep"), "tp"),
            P("tp", ("seq", "rep"), None),
            P("tp", ("seq", "rep"), None),
        ),
        check_vma=False,
    )
```

time: 391 us -> 62.7 us (0.16)
  matrix products: 182 us -> 0 us
  other arithmetic: 111 us -> 0 us
  waiting for transfers between devices: 66.9 us -> 0 us
  Pallas kernels: 0 us -> 56 us
  between operations: 14.2 us -> 1.29 us
    dot_general x66 -> x0, matrix products: 182 us -> none  [the longest x32 95.3 us: fold_block(): jnp.einsum('qegd,ned->egqn', queries, key_rows, preferred_element_type=jn...]
    reduce_sum x32 -> x0, other arithmetic: 73.1 us -> none  [fold_block(): new_sum = run_sum * factor + jnp.sum(weights, axis=-1)]
    all_gather x1 -> x0, waiting for transfers between devices: 66.9 us -> none  [on_device(): lax.all_gather(local_kv, ('seq', 'rep'), axis=0, tiled=True)]
    pallas_call x0 -> x1, Pallas kernels: none -> 56 us  [on_device(): pl.pallas_call(kernel, out_shape=(jax.ShapeDtypeStruct((QROWS, GROUPS * H...]
    lt x33 -> x0, other arithmetic: 21.4 us -> none  [the longest x32 21.3 us: fold_block(): ctx_pos[None, :] < valid_limit]
    select_n x33 -> x0, other arithmetic: 10.3 us -> none  [the longest x32 10.3 us: fold_block(): jnp.where(is_ctx[None, :], ctx_pos[None, :] < valid_limit, span_row[None,...]
  transfers between devices with their start and end apart: 2 -> 0, of which waited for: 1 -> 0; matrix products, arithmetic and copies ran while one was open for 2% -> 0% of each run, Pallas kernels for 0% -> 0%
where the time goes in v1:
time: 62.7 us; the launch traced here: 61.8 us
  Pallas kernels  56 us (89%)
  local copies, waits for them, and re-layouts  4.47 us (7%)
  between operations  1.29 us (2%)
    pallas_call x1, Pallas kernels, on_device(): pl.pallas_call(kernel, out_shape=(jax.ShapeDtypeStruct((QROWS, GROUPS * H...  56 us
    unnamed x3, local copies, waits for them, and re-layouts  4.47 us

profile of v1, /device:TPU:1, one launch (start us, length us, event | category | flops | bytes accessed | tf_op | source)
XLA Modules:
  0.0 61.8 jit_solution(2028550230725463513)
XLA Ops:
  1.3 56.0 %shard_map.130 = (bf16[128,1024]{1,0:T(8,128)(2,1)}, bf16[1,64,512]{2,1,0:T(8,128)(2,1)}, bf16[1,4,2048]{2,1,0:T(4,128)(2,1)}) custom-call(bf16[128,1024]{1,0:T(8,128)(2,1)} %query.1, bf16[128,128]{1,0:T(8,128)(2,1)} %key_span.1, bf16[128,128]{1,0:T(8,128)(2,1)} %value_span.1, bf16[512,128]{1,0:T(8,128)(2,1)} %ctx_k.1, bf16[512,128]{1,0:T(8,128)(2,1)} %ctx_v.1, ...), custom_call_target="tpu_custom_call" | custom-call | flops 12000000000 | bytes 8000000 | tf_op jit(solution)/shard_map/pallas_call | solution.py:398
  57.3 1.7 %copy.18 = bf16[128,1024]{1,0:T(8,128)(2,1)} copy(bf16[128,1024]{1,0:T(8,128)(2,1)} %get-tuple-element.6) | data formatting | bytes 524288
  59.0 1.5 %copy.19 = bf16[1,64,512]{2,1,0:T(8,128)(2,1)} copy(bf16[1,64,512]{2,1,0:T(8,128)(2,1)} %get-tuple-element.7) | data formatting | bytes 131072
  60.5 1.3 %copy.20 = bf16[1,4,2048]{2,1,0:T(4,128)(2,1)} copy(bf16[1,4,2048]{2,1,0:T(4,128)(2,1)} %get-tuple-element.8) | data formatting | bytes 32768

commit v2 on v1

v2 whole, which is shorter than its diff:
```python
import jax
import jax.numpy as jnp
from jax import lax
from jax.experimental import pallas as pl
from jax.experimental.pallas import tpu as pltpu
from jax.sharding import PartitionSpec as P

HD = 128
GROUPS = 8
QROWS = 128
CROWS = 512
SHARD = CROWS + QROWS
PIECE = SHARD // 2
Z = 8
SCALE2 = 1.4426950408889634 / 128**0.5
MASKED = -1e31
M_START = -1e29
ALL_ROWS = 2 * Z * SHARD
TILE = 256
MESH = pl.DeviceIdType.MESH
BF = jnp.bfloat16
F32 = jnp.float32

SLOT_OF = ((0, 1, 3, 5, 7), (0, 2, 4, 6, 7))

STEPS = (
    (0, 0, 1280),
    (1, 0, 1280),
    (1, 1280, 1280),
    (0, 1280, 1280),
    (1, 2560, 2560),
    (0, 2560, 2560),
    (1, 5120, 2560),
    (1, 7680, 2560),
    (0, 5120, 2560),
    (0, 7680, 2560),
)
DUTIES = {
    0: ((0, 1, 0), (1, (0,))),
    1: ((2,),),
    2: ((0, 1, 1),),
    4: ((0, 2, 0), (0, 2, 1), (1, (1, 2))),
    5: ((0, 3, 0),),
    6: ((0, 3, 1), (1, (3, 4))),
    7: ((0, 4, 0), (1, (5, 6, 7))),
}
SEND_AFTER = 7


def base_of(slot, theirs):
    if slot == 0:
        return theirs * SHARD
    if slot == 7:
        return 7 * 2 * SHARD + theirs * SHARD
    return 2 * SHARD + ((slot - 1) // 2) * 4 * SHARD + ((slot - 1) % 2) * SHARD + theirs * 2 * SHARD


def pick(i, table):
    total = jnp.int32(0)
    for at, value in enumerate(table):
        if value:
            total = total + jnp.where(i == at, jnp.int32(value), jnp.int32(0))
    return total


def kernel(
    query,
    key_span,
    value_span,
    ctx_k,
    ctx_v,
    offset,
    dec_q,
    lengths,
    slots,
    cache_k,
    cache_v,
    out_att,
    out_hand,
    out_dec,
    qb,
    kv,
    mask,
    ident,
    m_ref,
    acc_ref,
    o_send,
    o_recv,
    l_send,
    l_recv,
    hbuf,
    dqb,
    ckb,
    cvb,
    ring_send,
    ring_recv,
    core_send,
    core_recv,
    misc_send,
    misc_recv,
    local_sem,
):
    z = lax.axis_index("seq")
    tp = lax.axis_index("tp")
    rep = lax.axis_index("rep")
    y = rep // 2
    c = rep % 2
    half = tp // 4
    nxt = {"seq": (z + 1) % Z}
    prv = {"seq": (z + Z - 1) % Z}
    core = {"rep": y * 2 + (1 - c)}
    other = {"rep": (1 - y) * 2 + c}
    mate = {"tp": (1 - half) * 4 + tp % 4}

    def held(slot, theirs, part):
        return kv.at[pl.ds(base_of(slot, theirs) + part * PIECE, PIECE), :]

    def ring(way, hop, turn):
        part = turn if way == 0 else 1 - turn
        at = (way * 4 + hop - 1) * 2 + turn
        return pltpu.make_async_remote_copy(
            src_ref=held(SLOT_OF[way][hop - 1], 0, part),
            dst_ref=held(SLOT_OF[way][hop], 0, part),
            send_sem=ring_send.at[at],
            recv_sem=ring_recv.at[at],
            device_id=nxt if way == 0 else prv,
            device_id_type=MESH,
        )

    def has_hop(hop, turn):
        return hop <= 3 or (hop == 4 and turn == 0)

    def across(slot, part):
        at = slot * 2 + part
        return pltpu.make_async_remote_copy(
            src_ref=held(slot, 0, part),
            dst_ref=held(slot, 1, part),
            send_sem=core_send.at[at],
            recv_sem=core_recv.at[at],
            device_id=core,
            device_id_type=MESH,
        )

    def pass_on(hop, turn):
        for way in (0, 1):
            ring(way, hop, turn).wait_recv()
            if has_hop(hop + 1, turn):
                ring(way, hop + 1, turn).start()
            across(SLOT_OF[way][hop], turn if way == 0 else 1 - turn).start()

    def misc(at, src, dst, device):
        return pltpu.make_async_remote_copy(
            src_ref=src,
            dst_ref=dst,
            send_sem=misc_send.at[at],
            recv_sem=misc_recv.at[at],
            device_id=device,
            device_id_type=MESH,
        )

    q_copy = misc(0, qb.at[0], qb.at[1], other)
    kept = pl.ds(pl.multiple_of(half * 64, 64), 64)
    given = pl.ds(pl.multiple_of(CROWS + (1 - half) * 64, 64), 64)
    h_copy = misc(1, kv.at[given, :], hbuf.at[half], mate)
    o_copy = misc(2, o_send, o_recv, other)
    l_copy = misc(3, l_send, l_recv, other)

    def run(todo):
        for what in todo:
            if what[0] == 0:
                pass_on(what[1], what[2])
            elif what[0] == 1:
                for slot in what[1]:
                    for part in (0, 1):
                        across(slot, part).wait_recv()
            else:
                q_copy.wait_recv()

    left, right = pl.ds(0, HD), pl.ds(HD, HD)
    local = [
        pltpu.make_async_copy(src, dst, local_sem.at[at])
        for at, (src, dst) in enumerate(
            (
                (ctx_k, kv.at[pl.ds(0, CROWS), left]),
                (ctx_v, kv.at[pl.ds(0, CROWS), right]),
                (key_span, kv.at[pl.ds(CROWS, QROWS), left]),
                (value_span, kv.at[pl.ds(CROWS, QROWS), right]),
                (query, qb.at[0]),
                (dec_q.at[0], dqb),
                (cache_k.at[0], ckb),
                (cache_v.at[0], cvb),
                (key_span.at[kept, :], hbuf.at[half, :, left]),
                (value_span.at[kept, :], hbuf.at[half, :, right]),
            )
        )
    ]
    barrier = pltpu.get_barrier_semaphore()
    for device in (nxt, prv, core, other, mate):
        pl.semaphore_signal(barrier, inc=1, device_id=device, device_id_type=MESH)
    for copy in local:
        copy.start()
    for copy in local[:5]:
        copy.wait()
    pl.semaphore_wait(barrier, 5)

    for turn in (0, 1):
        for way in (0, 1):
            ring(way, 1, turn).start()
    for part in (0, 1):
        across(0, part).start()
    q_copy.start()
    h_copy.start()

    row = lax.broadcasted_iota(jnp.int32, (QROWS, HD), 0)
    col = lax.broadcasted_iota(jnp.int32, (QROWS, HD), 1)
    ident[...] = jnp.where(row == col, 1.0, 0.0).astype(BF)
    limit = offset[0]
    long_row = lax.broadcasted_iota(jnp.int32, (CROWS, HD), 0)

    def fill(slot, carry):
        odd = slot % 2
        z_slot = (z + 2 * Z - odd * ((slot + 1) // 2) + (1 - odd) * (slot // 2)) % Z
        for theirs in (0, 1):
            block = z_slot * 4 + y * 2 + (c if theirs == 0 else 1 - c)
            base = jnp.where(
                (slot > 0) & (slot < 7),
                2 * SHARD
                + ((slot + 1) // 2 - 1) * 4 * SHARD
                + (1 - odd) * SHARD
                + theirs * 2 * SHARD,
                slot * 2 * SHARD + theirs * SHARD,
            )
            base = pl.multiple_of(base, QROWS)
            long = jnp.where(long_row + block * CROWS >= limit, MASKED, 0.0).astype(BF)
            for b in (0, 1):
                y_b = y if b == 0 else 1 - y
                ahead = (block - (z * 4 + y_b * 2 + c)) * QROWS
                mask[b, pl.ds(base, CROWS), :] = long
                mask[b, pl.ds(base + CROWS, QROWS), :] = jnp.where(
                    row + ahead > col, MASKED, 0.0
                ).astype(BF)
        return carry

    lax.fori_loop(0, 8, fill, 0)
    m_ref[...] = jnp.full_like(m_ref, M_START)
    acc_ref[...] = jnp.zeros_like(acc_ref)

    for copy in local[5:]:
        copy.wait()
    dq = dqb[...].astype(F32)
    picked = [slots[half, b] for b in range(4)]
    live = [lengths[half, b] for b in range(4)]
    place = lax.broadcasted_iota(jnp.int32, (64, 512), 1)
    request = lax.broadcasted_iota(jnp.int32, (64, 512), 0) % 8
    ok = jnp.concatenate(
        [(request == b) & (place < live[b]) for b in range(4)], axis=1
    )
    blank = jnp.zeros((4, HD), F32)
    for head in (0, 1):
        lanes = slice(head * HD, (head + 1) * HD)
        q = jnp.concatenate(
            [
                part
                for g in range(GROUPS)
                for part in (dq[:, (head * 8 + g) * HD : (head * 8 + g + 1) * HD], blank)
            ],
            axis=0,
        ).astype(BF)
        k = jnp.concatenate([ckb[picked[b]][:, lanes] for b in range(4)], axis=0)
        v = jnp.concatenate([cvb[picked[b]][:, lanes] for b in range(4)], axis=0)
        s = lax.dot_general(q, k, (((1,), (1,)), ((), ())), preferred_element_type=F32)
        s = jnp.where(ok, s * SCALE2, MASKED)
        top = jnp.max(s, axis=1, keepdims=True)
        w = jnp.where(ok, jnp.exp2(s - top), 0.0)
        total = jnp.sum(w, axis=1, keepdims=True)
        o = lax.dot_general(
            w.astype(BF), v, (((1,), (0,)), ((), ())), preferred_element_type=F32
        )
        o = o / total
        for g in range(GROUPS):
            out_dec[0, :, (head * 8 + g) * HD : (head * 8 + g + 1) * HD] = o[
                g * 8 : g * 8 + 4, :
            ].astype(BF)

    def scores_block(b, key_off, width):
        keys = pl.ds(pl.multiple_of(key_off, 256), width)
        k = jnp.concatenate([kv[keys, :HD], mask[b, keys, :]], axis=1)
        v = jnp.concatenate([kv[keys, HD:], jnp.ones((width, HD), BF)], axis=1)
        eye = jnp.concatenate([ident[...]] * 2, axis=0)
        all_s = []
        for t in range(4):
            q = jnp.concatenate(
                [qb[b, :, (2 * t + u) * HD : (2 * t + u + 1) * HD] for u in (0, 1)], axis=0
            )
            q = jnp.concatenate([q, eye], axis=1)
            all_s.append(
                lax.dot_general(q, k, (((1,), (1,)), ((), ())), preferred_element_type=F32)
            )
        for t in range(4):
            s = all_s[t]
            at = pl.ds(t * TILE, TILE)
            before = m_ref[b, at, :]
            now = jnp.maximum(before, jnp.max(s, axis=1, keepdims=True) * SCALE2)
            factor = jnp.exp2(before - now)
            p = jnp.exp2(s * SCALE2 - now[:, :1])
            m_ref[b, at, :] = now
            pv = lax.dot_general(
                p.astype(BF), v, (((1,), (0,)), ((), ())), preferred_element_type=F32
            )
            acc_ref[b, at, :] = acc_ref[b, at, :] * jnp.concatenate([factor, factor], axis=1) + pv

    def one_step(i, carry):
        for step, todo in DUTIES.items():
            pl.when(i == step)(lambda todo=todo: run(todo))
        b = pick(i, [s[0] for s in STEPS])
        off = pick(i, [s[1] for s in STEPS])
        short = pick(i, [int(s[2] == 1280) for s in STEPS])
        pl.when(short == 1)(lambda: scores_block(b, off, 1280))
        pl.when(short == 0)(lambda: scores_block(b, off, 2560))

        @pl.when(i == SEND_AFTER)
        def _():
            eye = ident[...].astype(F32)
            for g in range(GROUPS):
                at = pl.ds(g * QROWS, QROWS)
                total = acc_ref[1, at, HD:]
                o_send[at, :] = (acc_ref[1, at, :HD] / total).astype(BF)
                level = m_ref[1, at, :] + jnp.log(total) * 1.4426950408889634
                l_send[g : g + 1, :] = jnp.sum(level * eye, axis=0, keepdims=True)
            l_copy.start()
            o_copy.start()

        return carry

    lax.fori_loop(0, len(STEPS), one_step, 0)

    h_copy.wait()
    for u in (0, 1):
        out_hand[0, :, u * 2 * HD : (u + 1) * 2 * HD] = hbuf[u]
    for hop in (1, 2, 3, 4):
        for turn in (0, 1):
            for way in (0, 1):
                if has_hop(hop, turn):
                    ring(way, hop, turn).wait_send()
    for slot in range(8):
        for part in (0, 1):
            across(slot, part).wait_send()
    q_copy.wait_send()
    l_copy.wait()
    o_copy.wait()
    eye = ident[...].astype(F32)
    for g in range(GROUPS):
        at = pl.ds(g * QROWS, QROWS)
        level = jnp.sum(eye * l_recv[g : g + 1, :], axis=1, keepdims=True)
        mine = m_ref[0, at, :]
        top = jnp.maximum(mine, level)
        w_mine = jnp.exp2(mine - top)
        w_other = jnp.exp2(level - top)
        total = acc_ref[0, at, HD:] * w_mine + w_other
        o = acc_ref[0, at, :HD] * w_mine + o_recv[at, :].astype(F32) * w_other
        out_att[:, g * HD : (g + 1) * HD] = (o / total).astype(BF)


def deliver(a, b, c, out_a, out_b, out_c):
    out_a[...] = a[...]
    out_b[...] = b[...]
    out_c[...] = c[...]


def on_device(*args):
    anywhere = pl.BlockSpec(memory_space=pl.ANY)
    vmem = pl.BlockSpec(memory_space=pltpu.VMEM)
    smem = pl.BlockSpec(memory_space=pltpu.SMEM)
    dma = pltpu.SemaphoreType.DMA
    shapes = (
        jax.ShapeDtypeStruct((QROWS, GROUPS * HD), BF),
        jax.ShapeDtypeStruct((1, 64, 512), BF),
        jax.ShapeDtypeStruct((1, 4, 2048), BF),
    )
    results = pl.pallas_call(
        kernel,
        out_shape=shapes,
        in_specs=[
            anywhere,
            anywhere,
            anywhere,
            anywhere,
            anywhere,
            smem,
            anywhere,
            smem,
            smem,
            anywhere,
            anywhere,
        ],
        out_specs=(vmem, vmem, vmem),
        scratch_shapes=[
            pltpu.VMEM((2, QROWS, GROUPS * HD), BF),
            pltpu.VMEM((ALL_ROWS, 2 * HD), BF),
            pltpu.VMEM((2, ALL_ROWS, HD), BF),
            pltpu.VMEM((QROWS, HD), BF),
            pltpu.VMEM((2, GROUPS * QROWS, HD), F32),
            pltpu.VMEM((2, GROUPS * QROWS, 2 * HD), F32),
            pltpu.VMEM((GROUPS * QROWS, HD), BF),
            pltpu.VMEM((GROUPS * QROWS, HD), BF),
            pltpu.VMEM((GROUPS, HD), F32),
            pltpu.VMEM((GROUPS, HD), F32),
            pltpu.VMEM((2, 64, 2 * HD), BF),
            pltpu.VMEM((4, 2048), BF),
            pltpu.VMEM((6, 512, 256), BF),
            pltpu.VMEM((6, 512, 256), BF),
            dma((16,)),
            dma((16,)),
            dma((16,)),
            dma((16,)),
            dma((4,)),
            dma((4,)),
            dma((10,)),
        ],
        compiler_params=pltpu.CompilerParams(
            collective_id=0, has_side_effects=True, vmem_limit_bytes=56 * 2**20
        ),
        cost_estimate=pl.CostEstimate(
            flops=12 * 10**9, bytes_accessed=8 * 10**6, transcendentals=22 * 10**6
        ),
    )(*args)
    return pl.pallas_call(
        deliver,
        out_shape=shapes,
        in_specs=[vmem] * 3,
        out_specs=(vmem,) * 3,
    )(*results)


def solution(mesh):
    placed = (
        P(("seq", "rep"), "tp"),
        P(("seq", "rep"), "tp"),
        P(("seq", "rep"), "tp"),
        P(("seq", "rep"), "tp"),
        P(("seq", "rep"), "tp"),
        P(),
        P("tp", ("seq", "rep"), None),
        P(None, ("seq", "rep")),
        P(None, ("seq", "rep")),
        P("tp", ("seq", "rep"), None, None),
        P("tp", ("seq", "rep"), None, None),
    )
    return jax.shard_map(
        on_device,
        mesh=mesh,
        in_specs=placed,
        out_specs=(
            P(("seq", "rep"), "tp"),
            P("tp", ("seq", "rep"), None),
            P("tp", ("seq", "rep"), None),
        ),
        check_vma=False,
    )
```

time: 62.7 us -> 54.2 us (0.86); the launches traced: 61.8 us -> 54.1 us
  local copies, waits for them, and re-layouts: 4.47 us -> 0 us
  Pallas kernels: 56 us -> 52.8 us
    unnamed x3 -> x0, local copies, waits for them, and re-layouts: 4.47 us -> none
    pallas_call x1 -> x2, Pallas kernels: 56 us -> 52.8 us  [the longest x1 51.1 us: on_device(): pl.pallas_call(kernel, out_shape=shapes, in_specs=[anywhere, anywhere, an...]
where the time goes in v2:
time: 54.2 us; the launch traced here: 54.1 us
  Pallas kernels  52.8 us (97%)
  between operations  1.29 us (2%)
    pallas_call x1, Pallas kernels, on_device(): pl.pallas_call(kernel, out_shape=shapes, in_specs=[anywhere, anywhere, an...  51.1 us
    pallas_call x1, Pallas kernels, on_device(): pl.pallas_call(deliver, out_shape=shapes, in_specs=[vmem] * 3, out_specs=...  1.72 us

profile of v2, /device:TPU:1, one launch (start us, length us, event | category | flops | bytes accessed | tf_op | source)
XLA Modules:
  0.0 54.1 jit_solution(11723255142652481502)
XLA Ops:
  1.3 51.1 %shard_map.130 = (bf16[128,1024]{1,0:T(8,128)(2,1)}, bf16[1,64,512]{2,1,0:T(8,128)(2,1)}, bf16[1,4,2048]{2,1,0:T(4,128)(2,1)}) custom-call(bf16[128,1024]{1,0:T(8,128)(2,1)} %query.1, bf16[128,128]{1,0:T(8,128)(2,1)} %key_span.1, bf16[128,128]{1,0:T(8,128)(2,1)} %value_span.1, bf16[512,128]{1,0:T(8,128)(2,1)} %ctx_k.1, bf16[512,128]{1,0:T(8,128)(2,1)} %ctx_v.1, ...), custom_call_target="tpu_custom_call" | custom-call | flops 12000000000 | bytes 8000000 | tf_op jit(solution)/shard_map/pallas_call | solution.py:380
  52.4 1.7 %shard_map.131 = (bf16[128,1024]{1,0:T(8,128)(2,1)}, bf16[1,64,512]{2,1,0:T(8,128)(2,1)}, bf16[1,4,2048]{2,1,0:T(4,128)(2,1)}) custom-call(bf16[128,1024]{1,0:T(8,128)(2,1)} %get-tuple-element.6.a, bf16[1,64,512]{2,1,0:T(8,128)(2,1)} %get-tuple-element.7.b, bf16[1,4,2048]{2,1,0:T(4,128)(2,1)} %get-tuple-element.8.c), custom_call_target="tpu_custom_call" | custom-call | tf_op jit(solution)/shard_map/pallas_call | solution.py:427

commit v3 on v2

--- a/solution.py
+++ b/solution.py
@@ -9,13 +9,12 @@
 GROUPS = 8
 QROWS = 128
 CROWS = 512
-SHARD = CROWS + QROWS
-PIECE = SHARD // 2
+PIECE = CROWS // 2
 Z = 8
 SCALE2 = 1.4426950408889634 / 128**0.5
 MASKED = -1e31
 M_START = -1e29
-ALL_ROWS = 2 * Z * SHARD
+ALL_ROWS = 2 * Z * (CROWS + QROWS)
 TILE = 256
 MESH = pl.DeviceIdType.MESH
 BF = jnp.bfloat16
@@ -24,35 +23,49 @@
 SLOT_OF = ((0, 1, 3, 5, 7), (0, 2, 4, 6, 7))
 
 STEPS = (
-    (0, 0, 1280),
-    (1, 0, 1280),
-    (1, 1280, 1280),
-    (0, 1280, 1280),
-    (1, 2560, 2560),
-    (0, 2560, 2560),
-    (1, 5120, 2560),
-    (1, 7680, 2560),
-    (0, 5120, 2560),
-    (0, 7680, 2560),
+    (0, 0, 1280, -1),
+    (1, 0, 1280, -1),
+    (1, 1280, 1280, 0),
+    (0, 1280, 1280, 0),
+    (1, 2560, 2560, 0),
+    (0, 2560, 2560, 0),
+    (1, 5120, 2560, 1),
+    (1, 7680, 2560, 2),
+    (0, 5120, 2560, 1),
+    (0, 7680, 2560, 2),
 )
 DUTIES = {
     0: ((0, 1, 0), (1, (0,))),
-    1: ((2,),),
+    1: ((3, 1), (2,)),
     2: ((0, 1, 1),),
-    4: ((0, 2, 0), (0, 2, 1), (1, (1, 2))),
-    5: ((0, 3, 0),),
+    4: ((0, 2, 0), (3, 2), (0, 2, 1), (1, (1, 2))),
+    5: ((0, 3, 0), (3, 3)),
     6: ((0, 3, 1), (1, (3, 4))),
-    7: ((0, 4, 0), (1, (5, 6, 7))),
+    7: ((0, 4, 0), (3, 4), (1, (5, 6, 7))),
 }
 SEND_AFTER = 7
 
 
 def base_of(slot, theirs):
     if slot == 0:
-        return theirs * SHARD
+        return theirs * 512
     if slot == 7:
-        return 7 * 2 * SHARD + theirs * SHARD
-    return 2 * SHARD + ((slot - 1) // 2) * 4 * SHARD + ((slot - 1) % 2) * SHARD + theirs * 2 * SHARD
+        return 8704 + theirs * 512
+    pair, second = (slot - 1) // 2, (slot - 1) % 2
+    if theirs:
+        return 2560 * (pair + 1) + second * 512
+    return (1280 if pair == 0 else 2560 * pair + 1024) + second * 512
+
+
+def span_base_of(slot, theirs):
+    if slot == 0:
+        return 1024 + theirs * 128
+    if slot == 7:
+        return 9984 + theirs * 128
+    pair, second = (slot - 1) // 2, (slot - 1) % 2
+    if theirs:
+        return 2560 * (pair + 1) + 2048 + second * 128
+    return 2304 + 2560 * pair + second * 128
 
 
 def pick(i, table):
@@ -96,6 +109,10 @@
     ring_recv,
     core_send,
     core_recv,
+    span_send,
+    span_recv,
+    pair_send,
+    pair_recv,
     misc_send,
     misc_recv,
     local_sem,
@@ -148,6 +165,54 @@
                 ring(way, hop + 1, turn).start()
             across(SLOT_OF[way][hop], turn if way == 0 else 1 - turn).start()
 
+    def span_rows(slot, theirs):
+        return kv.at[pl.ds(span_base_of(slot, theirs), QROWS), :]
+
+    def span_ring(way, hop):
+        return pltpu.make_async_remote_copy(
+            src_ref=span_rows(SLOT_OF[way][hop - 1], 0),
+            dst_ref=span_rows(SLOT_OF[way][hop], 0),
+            send_sem=span_send.at[way * 4 + hop - 1],
+            recv_sem=span_recv.at[way * 4 + hop - 1],
+            device_id=nxt if way == 0 else prv,
+            device_id_type=MESH,
+        )
+
+    def span_comes(way, hop):
+        return z >= hop if way == 0 else (z + hop) % Z <= 2
+
+    def span_goes(way, hop):
+        return (z + 1) % Z >= hop if way == 0 else (z + hop - 1) % Z <= 2
+
+    def span_hops():
+        return [(0, 1), (1, 1), (0, 2), (1, 2), (0, 3), (1, 3), (0, 4)]
+
+    def span_across(way, hop):
+        slot = SLOT_OF[way][hop]
+        return pltpu.make_async_remote_copy(
+            src_ref=span_rows(slot, 0),
+            dst_ref=span_rows(slot, 1),
+            send_sem=pair_send.at[slot],
+            recv_sem=pair_recv.at[slot],
+            device_id=core,
+            device_id_type=MESH,
+        )
+
+    def pass_span(hop):
+        for way in (0, 1):
+            if (way, hop) in span_hops():
+
+                @pl.when(span_comes(way, hop))
+                def _(way=way):
+                    span_ring(way, hop).wait_recv()
+                    span_across(way, hop).start()
+
+                if (way, hop + 1) in span_hops():
+
+                    @pl.when(span_goes(way, hop + 1))
+                    def _(way=way):
+                        span_ring(way, hop + 1).start()
+
     def misc(at, src, dst, device):
         return pltpu.make_async_remote_copy(
             src_ref=src,
@@ -160,7 +225,8 @@
 
     q_copy = misc(0, qb.at[0], qb.at[1], other)
     kept = pl.ds(pl.multiple_of(half * 64, 64), 64)
-    given = pl.ds(pl.multiple_of(CROWS + (1 - half) * 64, 64), 64)
+    mine = pl.ds(span_base_of(0, 0), QROWS)
+    given = pl.ds(pl.multiple_of(span_base_of(0, 0) + (1 - half) * 64, 64), 64)
     h_copy = misc(1, kv.at[given, :], hbuf.at[half], mate)
     o_copy = misc(2, o_send, o_recv, other)
     l_copy = misc(3, l_send, l_recv, other)
@@ -173,8 +239,19 @@
                 for slot in what[1]:
                     for part in (0, 1):
                         across(slot, part).wait_recv()
+                    if slot == 0:
+                        span_across(0, 0).wait_recv()
+                    for way, hop in span_hops():
+                        if SLOT_OF[way][hop] == slot:
+
+                            @pl.when(span_comes(way, hop))
+                            def _(way=way, hop=hop):
+                                span_across(way, hop).wait_recv()
+
+            elif what[0] == 2:
+                q_copy.wait_recv()
             else:
-                q_copy.wait_recv()
+                pass_span(what[1])
 
     left, right = pl.ds(0, HD), pl.ds(HD, HD)
     local = [
@@ -183,8 +260,8 @@
             (
                 (ctx_k, kv.at[pl.ds(0, CROWS), left]),
                 (ctx_v, kv.at[pl.ds(0, CROWS), right]),
-                (key_span, kv.at[pl.ds(CROWS, QROWS), left]),
-                (value_span, kv.at[pl.ds(CROWS, QROWS), right]),
+                (key_span, kv.at[mine, left]),
+                (value_span, kv.at[mine, right]),
                 (query, qb.at[0]),
                 (dec_q.at[0], dqb),
                 (cache_k.at[0], ckb),
@@ -203,11 +280,15 @@
         copy.wait()
     pl.semaphore_wait(barrier, 5)
 
-    for turn in (0, 1):
-        for way in (0, 1):
-            ring(way, 1, turn).start()
+    for way in (0, 1):
+        ring(way, 1, 0).start()
+    for way in (0, 1):
+        pl.when(span_goes(way, 1))(lambda way=way: span_ring(way, 1).start())
+    for way in (0, 1):
+        ring(way, 1, 1).start()
     for part in (0, 1):
         across(0, part).start()
+    span_across(0, 0).start()
     q_copy.start()
     h_copy.start()
 
@@ -217,31 +298,26 @@
     limit = offset[0]
     long_row = lax.broadcasted_iota(jnp.int32, (CROWS, HD), 0)
 
-    def fill(slot, carry):
-        odd = slot % 2
-        z_slot = (z + 2 * Z - odd * ((slot + 1) // 2) + (1 - odd) * (slot // 2)) % Z
+    for slot in range(8):
+        way, hop = (0, (slot + 1) // 2) if slot % 2 or slot == 0 else (1, slot // 2)
+        z_slot = (z + Z - hop) % Z if way == 0 else (z + hop) % Z
         for theirs in (0, 1):
             block = z_slot * 4 + y * 2 + (c if theirs == 0 else 1 - c)
-            base = jnp.where(
-                (slot > 0) & (slot < 7),
-                2 * SHARD
-                + ((slot + 1) // 2 - 1) * 4 * SHARD
-                + (1 - odd) * SHARD
-                + theirs * 2 * SHARD,
-                slot * 2 * SHARD + theirs * SHARD,
-            )
-            base = pl.multiple_of(base, QROWS)
+            far = pl.ds(base_of(slot, theirs), CROWS)
+            near = pl.ds(span_base_of(slot, theirs), QROWS)
             long = jnp.where(long_row + block * CROWS >= limit, MASKED, 0.0).astype(BF)
             for b in (0, 1):
                 y_b = y if b == 0 else 1 - y
                 ahead = (block - (z * 4 + y_b * 2 + c)) * QROWS
-                mask[b, pl.ds(base, CROWS), :] = long
-                mask[b, pl.ds(base + CROWS, QROWS), :] = jnp.where(
-                    row + ahead > col, MASKED, 0.0
-                ).astype(BF)
-        return carry
-
-    lax.fori_loop(0, 8, fill, 0)
+                mask[b, far, :] = long
+                mask[b, near, :] = jnp.where(row + ahead > col, MASKED, 0.0).astype(BF)
+
+            if slot:
+
+                @pl.when(jnp.logical_not(span_comes(way, hop)))
+                def _(near=near):
+                    kv[near, :] = jnp.zeros((QROWS, 2 * HD), BF)
+
     m_ref[...] = jnp.full_like(m_ref, M_START)
     acc_ref[...] = jnp.zeros_like(acc_ref)
 
@@ -314,9 +390,11 @@
             pl.when(i == step)(lambda todo=todo: run(todo))
         b = pick(i, [s[0] for s in STEPS])
         off = pick(i, [s[1] for s in STEPS])
-        short = pick(i, [int(s[2] == 1280) for s in STEPS])
-        pl.when(short == 1)(lambda: scores_block(b, off, 1280))
-        pl.when(short == 0)(lambda: scores_block(b, off, 2560))
+        width = pick(i, [s[2] for s in STEPS])
+        spare = pick(i, [s[3] + 1 for s in STEPS])
+        width = jnp.where(z < spare, (width // 5) * 4, width)
+        for size in (1024, 1280, 2048, 2560):
+            pl.when(width == size)(lambda size=size: scores_block(b, off, size))
 
         @pl.when(i == SEND_AFTER)
         def _():
@@ -345,6 +423,10 @@
     for slot in range(8):
         for part in (0, 1):
             across(slot, part).wait_send()
+    span_across(0, 0).wait_send()
+    for way, hop in span_hops():
+        pl.when(span_goes(way, hop))(lambda way=way, hop=hop: span_ring(way, hop).wait_send())
+        pl.when(span_comes(way, hop))(lambda way=way, hop=hop: span_across(way, hop).wait_send())
     q_copy.wait_send()
     l_copy.wait()
     o_copy.wait()
@@ -413,6 +495,10 @@
             dma((16,)),
             dma((16,)),
             dma((16,)),
+            dma((8,)),
+            dma((8,)),
+            dma((8,)),
+            dma((8,)),
             dma((4,)),
             dma((4,)),
             dma((10,)),

time: 54.2 us -> 50.8 us (0.937)
  Pallas kernels: 52.8 us -> 49.2 us
    pallas_call x1, Pallas kernels: 51.1 us -> 47.5 us  [on_device(): pl.pallas_call(kernel, out_shape=shapes, in_specs=[anywhere, anywhere, an...]
where the time goes in v3:
time: 50.8 us; the launch traced here: 50.5 us
  Pallas kernels  49.2 us (97%)
  between operations  1.29 us (3%)
    pallas_call x1, Pallas kernels, on_device(): pl.pallas_call(kernel, out_shape=shapes, in_specs=[anywhere, anywhere, an...  47.5 us
    pallas_call x1, Pallas kernels, on_device(): pl.pallas_call(deliver, out_shape=shapes, in_specs=[vmem] * 3, out_specs=...  1.72 us

profile of v3, /device:TPU:1, one launch (start us, length us, event | category | flops | bytes accessed | tf_op | source)
XLA Modules:
  0.0 50.5 jit_solution(18142058112706481642)
XLA Ops:
  1.3 47.5 %shard_map.130 = (bf16[128,1024]{1,0:T(8,128)(2,1)}, bf16[1,64,512]{2,1,0:T(8,128)(2,1)}, bf16[1,4,2048]{2,1,0:T(4,128)(2,1)}) custom-call(bf16[128,1024]{1,0:T(8,128)(2,1)} %query.1, bf16[128,128]{1,0:T(8,128)(2,1)} %key_span.1, bf16[128,128]{1,0:T(8,128)(2,1)} %value_span.1, bf16[512,128]{1,0:T(8,128)(2,1)} %ctx_k.1, bf16[512,128]{1,0:T(8,128)(2,1)} %ctx_v.1, ...), custom_call_target="tpu_custom_call" | custom-call | flops 12000000000 | bytes 8000000 | tf_op jit(solution)/shard_map/pallas_call | solution.py:462
  48.8 1.7 %shard_map.131 = (bf16[128,1024]{1,0:T(8,128)(2,1)}, bf16[1,64,512]{2,1,0:T(8,128)(2,1)}, bf16[1,4,2048]{2,1,0:T(4,128)(2,1)}) custom-call(bf16[128,1024]{1,0:T(8,128)(2,1)} %get-tuple-element.6.a, bf16[1,64,512]{2,1,0:T(8,128)(2,1)} %get-tuple-element.7.b, bf16[1,4,2048]{2,1,0:T(4,128)(2,1)} %get-tuple-element.8.c), custom_call_target="tpu_custom_call" | custom-call | tf_op jit(solution)/shard_map/pallas_call | solution.py:513

commit v4 on v3

--- a/solution.py
+++ b/solution.py
@@ -23,38 +23,43 @@
 SLOT_OF = ((0, 1, 3, 5, 7), (0, 2, 4, 6, 7))
 
 STEPS = (
-    (0, 0, 1280, -1),
-    (1, 0, 1280, -1),
-    (1, 1280, 1280, 0),
-    (0, 1280, 1280, 0),
-    (1, 2560, 2560, 0),
-    (0, 2560, 2560, 0),
-    (1, 5120, 2560, 1),
-    (1, 7680, 2560, 2),
-    (0, 5120, 2560, 1),
-    (0, 7680, 2560, 2),
+    (0, 0, 1280, -1, 0),
+    (1, 0, 1280, -1, 0),
+    (1, 1280, 1280, 0, 0),
+    (0, 1280, 1280, 0, 0),
+    (1, 2560, 1280, 0, 256),
+    (1, 3840, 1280, 1, 0),
+    (0, 2560, 2560, 0, 256),
+    (1, 5120, 1280, 1, 256),
+    (1, 6400, 1280, 2, 0),
+    (1, 7680, 1280, 2, 256),
+    (1, 8960, 1280, 3, 0),
+    (0, 5120, 2560, 1, 256),
+    (0, 7680, 2560, 2, 256),
 )
 DUTIES = {
-    0: ((0, 1, 0), (1, (0,))),
-    1: ((3, 1), (2,)),
+    0: ((1, (0,)),),
+    1: ((0, 1, 0), (3, 1), (2,)),
     2: ((0, 1, 1),),
-    4: ((0, 2, 0), (3, 2), (0, 2, 1), (1, (1, 2))),
-    5: ((0, 3, 0), (3, 3)),
-    6: ((0, 3, 1), (1, (3, 4))),
-    7: ((0, 4, 0), (3, 4), (1, (5, 6, 7))),
+    4: ((0, 2, 0), (3, 2), (1, (1, 2))),
+    5: ((0, 2, 1),),
+    7: ((0, 3, 0), (3, 3), (1, (3, 4))),
+    8: ((0, 3, 1),),
+    9: ((0, 4, 0), (1, (5, 6))),
+    10: ((3, 4), (1, (7,))),
 }
-SEND_AFTER = 7
+SEND_AFTER = 10
 
 
 def base_of(slot, theirs):
     if slot == 0:
         return theirs * 512
     if slot == 7:
-        return 8704 + theirs * 512
+        return 8960 + theirs * 512
     pair, second = (slot - 1) // 2, (slot - 1) % 2
     if theirs:
-        return 2560 * (pair + 1) + second * 512
-    return (1280 if pair == 0 else 2560 * pair + 1024) + second * 512
+        return 2560 * (pair + 1) + 256 + second * 512
+    return 1280 + 2560 * pair + second * 512
 
 
 def span_base_of(slot, theirs):
@@ -64,7 +69,7 @@
         return 9984 + theirs * 128
     pair, second = (slot - 1) // 2, (slot - 1) % 2
     if theirs:
-        return 2560 * (pair + 1) + 2048 + second * 128
+        return 2560 * (pair + 1) + second * 128
     return 2304 + 2560 * pair + second * 128
 
 
@@ -228,8 +233,11 @@
     mine = pl.ds(span_base_of(0, 0), QROWS)
     given = pl.ds(pl.multiple_of(span_base_of(0, 0) + (1 - half) * 64, 64), 64)
     h_copy = misc(1, kv.at[given, :], hbuf.at[half], mate)
-    o_copy = misc(2, o_send, o_recv, other)
-    l_copy = misc(3, l_send, l_recv, other)
+    half_rows = [pl.ds(h * 4 * QROWS, 4 * QROWS) for h in (0, 1)]
+    o_copies = [
+        misc(2 + h, o_send.at[half_rows[h], :], o_recv.at[half_rows[h], :], other) for h in (0, 1)
+    ]
+    l_copies = [misc(4 + h, l_send.at[h], l_recv.at[h], other) for h in (0, 1)]
 
     def run(todo):
         for what in todo:
@@ -392,6 +400,7 @@
         off = pick(i, [s[1] for s in STEPS])
         width = pick(i, [s[2] for s in STEPS])
         spare = pick(i, [s[3] + 1 for s in STEPS])
+        off = off + jnp.where(z < spare, pick(i, [s[4] for s in STEPS]), 0)
         width = jnp.where(z < spare, (width // 5) * 4, width)
         for size in (1024, 1280, 2048, 2560):
             pl.when(width == size)(lambda size=size: scores_block(b, off, size))
@@ -399,14 +408,15 @@
         @pl.when(i == SEND_AFTER)
         def _():
             eye = ident[...].astype(F32)
-            for g in range(GROUPS):
-                at = pl.ds(g * QROWS, QROWS)
-                total = acc_ref[1, at, HD:]
-                o_send[at, :] = (acc_ref[1, at, :HD] / total).astype(BF)
-                level = m_ref[1, at, :] + jnp.log(total) * 1.4426950408889634
-                l_send[g : g + 1, :] = jnp.sum(level * eye, axis=0, keepdims=True)
-            l_copy.start()
-            o_copy.start()
+            for h in (0, 1):
+                for g in range(4):
+                    at = pl.ds((h * 4 + g) * QROWS, QROWS)
+                    total = acc_ref[1, at, HD:]
+                    o_send[at, :] = (acc_ref[1, at, :HD] / total).astype(BF)
+                    level = m_ref[1, at, :] + jnp.log(total) * 1.4426950408889634
+                    l_send[h, g : g + 1, :] = jnp.sum(level * eye, axis=0, keepdims=True)
+                l_copies[h].start()
+                o_copies[h].start()
 
         return carry
 
@@ -428,19 +438,21 @@
         pl.when(span_goes(way, hop))(lambda way=way, hop=hop: span_ring(way, hop).wait_send())
         pl.when(span_comes(way, hop))(lambda way=way, hop=hop: span_across(way, hop).wait_send())
     q_copy.wait_send()
-    l_copy.wait()
-    o_copy.wait()
     eye = ident[...].astype(F32)
-    for g in range(GROUPS):
-        at = pl.ds(g * QROWS, QROWS)
-        level = jnp.sum(eye * l_recv[g : g + 1, :], axis=1, keepdims=True)
-        mine = m_ref[0, at, :]
-        top = jnp.maximum(mine, level)
-        w_mine = jnp.exp2(mine - top)
-        w_other = jnp.exp2(level - top)
-        total = acc_ref[0, at, HD:] * w_mine + w_other
-        o = acc_ref[0, at, :HD] * w_mine + o_recv[at, :].astype(F32) * w_other
-        out_att[:, g * HD : (g + 1) * HD] = (o / total).astype(BF)
+    for h in (0, 1):
+        l_copies[h].wait()
+        o_copies[h].wait()
+        for g in range(4):
+            head = h * 4 + g
+            at = pl.ds(head * QROWS, QROWS)
+            level = jnp.sum(eye * l_recv[h, g : g + 1, :], axis=1, keepdims=True)
+            mine = m_ref[0, at, :]
+            top = jnp.maximum(mine, level)
+            w_mine = jnp.exp2(mine - top)
+            w_other = jnp.exp2(level - top)
+            total = acc_ref[0, at, HD:] * w_mine + w_other
+            o = acc_ref[0, at, :HD] * w_mine + o_recv[at, :].astype(F32) * w_other
+            out_att[:, head * HD : (head + 1) * HD] = (o / total).astype(BF)
 
 
 def deliver(a, b, c, out_a, out_b, out_c):
@@ -485,8 +497,8 @@
             pltpu.VMEM((2, GROUPS * QROWS, 2 * HD), F32),
             pltpu.VMEM((GROUPS * QROWS, HD), BF),
             pltpu.VMEM((GROUPS * QROWS, HD), BF),
-            pltpu.VMEM((GROUPS, HD), F32),
-            pltpu.VMEM((GROUPS, HD), F32),
+            pltpu.VMEM((2, 4, HD), F32),
+            pltpu.VMEM((2, 4, HD), F32),
             pltpu.VMEM((2, 64, 2 * HD), BF),
             pltpu.VMEM((4, 2048), BF),
             pltpu.VMEM((6, 512, 256), BF),
@@ -499,8 +511,8 @@
             dma((8,)),
             dma((8,)),
             dma((8,)),
-            dma((4,)),
-            dma((4,)),
+            dma((6,)),
+            dma((6,)),
             dma((10,)),
         ],
         compiler_params=pltpu.CompilerParams(

time: 50.8 us -> 50.6 us (level)
  no operation moved by 1% of the time
where the time goes in v4:
time: 50.6 us; the launch traced here: 50.5 us
  Pallas kernels  49.2 us (97%)
  between operations  1.29 us (3%)
    pallas_call x1, Pallas kernels, on_device(): pl.pallas_call(kernel, out_shape=shapes, in_specs=[anywhere, anywhere, an...  47.5 us
    pallas_call x1, Pallas kernels, on_device(): pl.pallas_call(deliver, out_shape=shapes, in_specs=[vmem] * 3, out_specs=...  1.72 us

profile of v4, /device:TPU:1, one launch (start us, length us, event | category | flops | bytes accessed | tf_op | source)
XLA Modules:
  0.0 50.5 jit_solution(16805649037725086433)
XLA Ops:
  1.3 47.5 %shard_map.130 = (bf16[128,1024]{1,0:T(8,128)(2,1)}, bf16[1,64,512]{2,1,0:T(8,128)(2,1)}, bf16[1,4,2048]{2,1,0:T(4,128)(2,1)}) custom-call(bf16[128,1024]{1,0:T(8,128)(2,1)} %query.1, bf16[128,128]{1,0:T(8,128)(2,1)} %key_span.1, bf16[128,128]{1,0:T(8,128)(2,1)} %value_span.1, bf16[512,128]{1,0:T(8,128)(2,1)} %ctx_k.1, bf16[512,128]{1,0:T(8,128)(2,1)} %ctx_v.1, ...), custom_call_target="tpu_custom_call" | custom-call | flops 12000000000 | bytes 8000000 | tf_op jit(solution)/shard_map/pallas_call | solution.py:474
  48.8 1.7 %shard_map.131 = (bf16[128,1024]{1,0:T(8,128)(2,1)}, bf16[1,64,512]{2,1,0:T(8,128)(2,1)}, bf16[1,4,2048]{2,1,0:T(4,128)(2,1)}) custom-call(bf16[128,1024]{1,0:T(8,128)(2,1)} %get-tuple-element.6.a, bf16[1,64,512]{2,1,0:T(8,128)(2,1)} %get-tuple-element.7.b, bf16[1,4,2048]{2,1,0:T(4,128)(2,1)} %get-tuple-element.8.c), custom_call_target="tpu_custom_call" | custom-call | tf_op jit(solution)/shard_map/pallas_call | solution.py:525
